TPU v7x, 128 devices: a whole 4x4x4 slice. The times are simulated.
128 devices in a mesh: var: 4 (over z), samp: 32 (over x, y, core).
Axes of the slice: x: 4, y: 4, z: 4, core: 2. Of those that a mesh axis runs over, the one named last changes fastest.
Arguments:
- genotypes: int32 [3072, 98304], P('var', 'samp'), may hold values from 0 to 2, as said below
- called: int32 [3072, 98304], P('var', 'samp'), may hold values from 0 to 1
- dosage: int32 [98304, 1024], P(('samp', 'var')), may hold values from 0 to 200
- sample_order: int32 [128, 768], P(('samp', 'var')), may hold values from 0 to 767, each once within a row
- noise_ratio: float32 [16], replicated, may hold values from 0.5 to 4
- solution: float32 [98304, 16], P(('samp', 'var')), may hold values from -13 to 13
- residual: float32 [98304, 16], P(('samp', 'var')), may hold values from -13 to 13
- direction: float32 [98304, 16], P(('samp', 'var')), may hold values from -13 to 13
Outputs:
- solution_new: float32 [98304, 16], P(('samp', 'var'))
- residual_new: float32 [98304, 16], P(('samp', 'var'))
- direction_new: float32 [98304, 16], P(('samp', 'var'))
- scores: float32 [1024, 16], P(('var', 'samp'))
Inputs may be any that keep to these rules, and one draw needn't show every extreme that they name: `genotypes`: where called is 1, the count of one allele. `sample_order`: each row lists 0 to 767 once.
All inputs are finite; a program needn't handle non-finite values.
Results may differ from a plain program's by a relative error of at most 0.023.
Values may be sent and summed in bfloat16 or wider, within the bound.
A program may use at most 128 MiB of HBM per device.

v0:
```python
import math

import jax
import jax.numpy as jnp
from jax import lax
from jax.sharding import PartitionSpec as P

VARIANTS = 3072


def standard_form(raw_proj, called_proj, allele_sum, called_count):
    frequency = (allele_sum + 1.0) / (2.0 * called_count + 2.0)
    spread = jnp.sqrt(2.0 * frequency * (1.0 - frequency))
    loading = (raw_proj - 2.0 * frequency[:, None] * called_proj) / spread[:, None]
    return (frequency, spread, loading)


def body(genotypes, called, dosage, sample_order, noise_ratio, solution, residual, direction):
    coded = genotypes * called
    coded_b = coded.astype(jnp.bfloat16)
    called_b = called.astype(jnp.bfloat16)
    allele_sum = jnp.sum(coded, axis=1).astype(jnp.float32)
    called_count = jnp.sum(called, axis=1).astype(jnp.float32)
    quarter = direction.shape[0]
    samples = quarter * lax.axis_size("samp") * lax.axis_size("var")
    dosage_b = dosage.astype(jnp.bfloat16)
    dosage_sum = jnp.sum(dosage, axis=0).astype(jnp.float32)
    order_row = sample_order[0]
    direction_b = direction.astype(jnp.bfloat16)
    piece = lax.all_gather(direction_b, "var", axis=0, tiled=True)
    coded_cols = coded_b
    called_cols = called_b
    raw_proj = jnp.dot(coded_cols, piece, preferred_element_type=jnp.float32)
    called_proj = jnp.dot(called_cols, piece, preferred_element_type=jnp.float32)
    raw_proj, called_proj, allele_sum, called_count = (
        lax.psum(raw_proj.astype(jnp.bfloat16), "samp").astype(jnp.float32),
        lax.psum(called_proj.astype(jnp.bfloat16), "samp").astype(jnp.float32),
        lax.psum(allele_sum.astype(jnp.bfloat16), "samp").astype(jnp.float32),
        lax.psum(called_count.astype(jnp.bfloat16), "samp").astype(jnp.float32),
    )
    frequency, spread, loading = standard_form(raw_proj, called_proj, allele_sum, called_count)
    scaled_a = (loading / spread[:, None]).astype(jnp.bfloat16)
    scaled_b = (2.0 * frequency[:, None] * loading / spread[:, None]).astype(jnp.bfloat16)
    coded_cols = coded_b
    called_cols = called_b
    term = jnp.einsum("vs,vc->sc", coded_cols, scaled_a, preferred_element_type=jnp.float32)
    term = term - jnp.einsum("vs,vc->sc", called_cols, scaled_b, preferred_element_type=jnp.float32)
    back = lax.psum_scatter(
        (term / VARIANTS).astype(jnp.bfloat16), "var", scatter_dimension=0, tiled=True
    ).astype(jnp.float32)
    applied = noise_ratio[None, :] * direction + back
    res_norm, curvature = lax.psum(
        (jnp.sum(residual * residual, axis=0), jnp.sum(direction * applied, axis=0)),
        ("var", "samp"),
    )
    step_size = res_norm / (curvature + 1e-06)
    solution_new = solution + step_size[None, :] * direction
    residual_new = residual - step_size[None, :] * applied
    res_square = jnp.sum(residual_new * residual_new, axis=0)
    res_new_norm, sol_sum, sol_square = lax.psum(
        (res_square, jnp.sum(solution_new, axis=0), jnp.sum(solution_new * solution_new, axis=0)),
        ("var", "samp"),
    )
    picked = jnp.take(solution_new, order_row, axis=0).astype(jnp.bfloat16)
    cross_local = jnp.einsum("ij,ic->jc", dosage_b, picked, preferred_element_type=jnp.float32)
    cross_sum, dosage_sum = (
        lax.psum_scatter(cross_local, ("var", "samp"), scatter_dimension=0, tiled=True),
        lax.psum_scatter(dosage_sum, ("var", "samp"), scatter_dimension=0, tiled=True),
    )
    direction_new = residual_new + (res_new_norm / (res_norm + 1e-06))[None, :] * direction
    dose_freq = (dosage_sum / 100.0 + 1.0) / (2.0 * samples + 2.0)
    dose_spread = jnp.sqrt(2.0 * dose_freq * (1.0 - dose_freq))
    scale_norm = math.sqrt(samples) * jnp.sqrt(sol_square / samples + 1e-06)
    scores = (cross_sum / 100.0 - 2.0 * dose_freq[:, None] * sol_sum[None, :]) / (
        dose_spread[:, None] * scale_norm[None, :]
    )
    return (solution_new, residual_new, direction_new, scores)


def solution(mesh):
    placed = (
        P("var", "samp"),
        P("var", "samp"),
        P(("samp", "var"), None),
        P(("samp", "var"), None),
        P(),
        P(("samp", "var"), None),
        P(("samp", "var"), None),
        P(("samp", "var"), None),
    )
    return jax.shard_map(
        body,
        mesh=mesh,
        in_specs=placed,
        out_specs=(
            P(("samp", "var"), None),
            P(("samp", "var"), None),
            P(("samp", "var"), None),
            P(("var", "samp"), None),
        ),
        check_vma=False,
    )
```

profile of v0, /device:TPU:1, one launch (start us, length us, event | category | flops | bytes accessed | tf_op | source)
XLA Modules:
  0.0 401.3 jit_solution(4430301488992100264)
XLA Ops:
  7.2 0.8 convert_element_type.61
  8.0 11.4 %all_gather.3 = bf16[3072,16]{0,1:T(8,128)(2,1)S(1)} all-gather(bf16[768,16]{0,1:T(8,128)(2,1)S(1)} %convert_element_type.61), channel_id=1, replica_groups=mesh['var'=4,'samp'=32] {'var'}, dimensions={0}, use_global_device_ids=true | all-gather | bytes 122880 | tf_op jit(solution)/shard_map/all_gather | solution.py:30
  19.5 10.1 %multiply_reduce_fusion = (s32[768]{0:T(1024)S(1)}, s32[768]{0:T(1024)S(1)}, bf16[768,3072]{1,0:T(8,128)(2,1)}) fusion(s32[768,3072]{1,0:T(8,128)} %param.8, s32[768,3072]{1,0:T(8,128)} %param.9), kind=kLoop, calls=%fused_computation.1 | loop fusion | flops 9435648 | bytes 23599104 | tf_op jit(solution)/shard_map/reduce_sum | solution.py:22
  29.6 5.1 %fusion.10 = bf16[768,16]{0,1:T(8,128)(2,1)S(1)} fusion(bf16[3072,16]{0,1:T(8,128)(2,1)S(1)} %all_gather.3, s32[768,3072]{1,0:T(8,128)} %param.9), kind=kOutput, calls=%fused_computation.13 | convolution fusion | flops 77869056 | bytes 9560064 | tf_op jit(solution)/shard_map/dot_general | solution.py:34
  34.7 1.3 convolution_convert_fusion
  36.1 123.5 %all-reduce.4 = (bf16[768,16]{0,1:T(8,128)(2,1)S(1)}, bf16[768,16]{0,1:T(8,128)(2,1)S(1)}, bf16[768]{0:T(1024)(128)(2,1)S(1)}, bf16[768]{0:T(1024)(128)(2,1)S(1)}) all-reduce(bf16[768,16]{0,1:T(8,128)(2,1)S(1)} %fusion.10, bf16[768,16]{0,1:T(8,128)(2,1)S(1)} %convolution_convert_fusion, ...), channel_id=1, replica_groups=mesh['var'=4,'samp'=32] {'samp'}, use_global_device_ids=true, to_apply=%region_7.0 | all-reduce | flops 26112 | bytes 104448 | tf_op jit(solution)/shard_map/psum | solution.py:37
  159.6 4.6 %convolution_bitcast_fusion = f32[3072,16]{0,1:T(8,128)S(1)} fusion(s32[768,3072]{1,0:T(8,128)} %param.9, bf16[768,16]{0,1:T(8,128)(2,1)S(1)} %get-tuple-element.26, bf16[768,16]{0,1:T(8,128)(2,1)S(1)} %get-tuple-element.27, f32[768]{0:T(1024)S(1)} %get-tuple-element.40, f32[768]{0:T(1024)S(1)} %get-tuple-element.41), kind=kOutput, calls=%fused_computation.5 | convolution fusion | flops 77955072 | bytes 9689088 | tf_op jit(solution)/shard_map/vs,vc->sc/dot_general | solution.py:47
  164.2 0.3 slice-done.1
  164.5 1.4 fusion.1
  166.1 2.3 reduce_sum.77
  168.4 16.6 %reduce-scatter.3.cloned.1.call-done = bf16[768,16]{0,1:T(8,128)(2,1)} async-done(((bf16[3072,16]{0,1:T(8,128)(2,1)}), bf16[768,16]{0,1:T(8,128)(2,1)}) %reduce-scatter.3.cloned.1.call-update) | async-done | bytes 24592 | tf_op jit(solution)/shard_map/reduce_scatter | solution.py:48
  185.0 0.9 multiply_reduce_fusion.3
  186.0 66.8 %all-reduce.3 = (f32[16]{0:T(128)S(1)}, f32[16]{0:T(128)S(1)}) all-reduce(f32[16]{0:T(128)S(1)} %multiply_reduce_fusion.4, f32[16]{0:T(128)S(1)} %multiply_reduce_fusion.3), channel_id=1, replica_groups=mesh['var'=4,'samp'=32] {'var','samp'}, use_global_device_ids=true, to_apply=%region_1.0 | all-reduce | flops 32 | bytes 256 | tf_op jit(solution)/shard_map/psum | solution.py:52
  252.8 2.1 multiply_reduce_fusion.2
  254.9 0.6 copy-done.4
  255.5 0.2 copy.16
  255.7 1.9 gather_fusion
  257.6 1.1 fusion.7
  258.7 63.2 %all-reduce.2 = (f32[16]{0:T(128)S(1)}, f32[16]{0:T(128)S(1)}, f32[1024]{0:T(1024)S(1)}, f32[16]{0:T(128)S(1)}) all-reduce(f32[16]{0:T(128)S(1)} %get-tuple-element.31, f32[16]{0:T(128)} %get-tuple-element.34, f32[1024]{0:T(1024)S(1)} %convert_element_type.79, f32[16]{0:T(128)} %get-tuple-element.35), channel_id=1, replica_groups=mesh['var'=4,'samp'=32] {'var','samp'}, use_global_device_ids=true, to_apply=%region_12.0 | all-reduce | flops 1072 | bytes 8576 | tf_op jit(solution)/shard_map/psum | solution.py:60
  321.9 0.6 add_divide_fusion.1
  322.6 1.5 multiply_add_fusion
  324.2 68.9 %all-reduce.7.cloned.1.call-done = f32[1024,16]{0,1:T(8,128)} async-done(((f32[1024,16]{0,1:T(8,128)}), f32[1024,16]{0,1:T(8,128)}) %all-reduce.7.cloned.1.call-update) | async-done | bytes 65552
  393.0 0.8 fusion.20
  393.8 0.7 copy.17
  (36 shorter events, 0.4 us)
Async XLA Ops:
  7.2 177.9 %reduce-scatter.3.cloned.1.call-start = ((), (), s32[]{:S(2)}) async-start(), calls=%async_computation.1 | async-start | bytes 122880 | tf_op jit(solution)/shard_map/reduce_scatter | solution.py:48
  29.6 5.2 %copy-start = (bf16[768,3072]{1,0:T(8,128)(2,1)S(1)}, bf16[768,3072]{1,0:T(8,128)(2,1)}, u32[]{:S(2)}) copy-start(bf16[768,3072]{1,0:T(8,128)(2,1)} %get-tuple-element.33) | copy-start | bytes 14155780
  34.7 129.5 %slice-start = ((s8[4718592]{0:T(1024)(128)(4,1)}), s8[524288]{0:T(1024)(128)(4,1)S(1)}, s32[]{:S(2)}) async-start(s8[4718592]{0:T(1024)(128)(4,1)} %bitcast.12), calls=%async_computation.3 | async-start | bytes 1048576
  159.6 4.9 %slice-start.1 = ((s8[4718592]{0:T(1024)(128)(4,1)}), s8[4194304]{0:T(1024)(128)(4,1)S(1)}, s32[]{:S(2)}) async-start(s8[4718592]{0:T(1024)(128)(4,1)} %bitcast.12), calls=%async_computation.4 | async-start | bytes 8388608
  164.2 1.8 copy-start.3
  164.2 1.9 copy-start.6
  164.2 20.9 %copy-start.2 = (f32[768,16]{0,1:T(8,128)S(1)}, f32[768,16]{0,1:T(8,128)}, u32[]{:S(2)}) copy-start(f32[768,16]{0,1:T(8,128)} %param.15) | copy-start | bytes 147460
  164.2 20.9 %copy-start.7 = (f32[16]{0:T(128)S(1)}, f32[16]{0:T(128)}, u32[]{:S(2)}) copy-start(f32[16]{0:T(128)} %param.12) | copy-start | bytes 196
  164.2 88.6 %copy-start.5 = (f32[768,16]{0,1:T(8,128)S(1)}, f32[768,16]{0,1:T(8,128)}, u32[]{:S(2)}) copy-start(f32[768,16]{0,1:T(8,128)} %param.13) | copy-start | bytes 147460
  165.8 91.7 %copy-start.1 = (s32[768,1024]{1,0:T(8,128)S(1)}, s32[768,1024]{1,0:T(8,128)}, u32[]{:S(2)}) copy-start(s32[768,1024]{1,0:T(8,128)} %param.10) | copy-start | bytes 9437188
  165.9 227.2 %all-reduce.7.cloned.1.call-start = ((), (), s32[]{:S(2)}) async-start(), calls=%async_computation.2 | async-start | bytes 131072
  252.8 2.1 copy-start.8
  254.9 0.6 copy-start.4
Sparse Core Ops, SparseCore 0:
  166.0 19.0 reduce-scatter.2
  258.8 134.1 all-reduce.6
where the time goes:
time: 402 us; the launch traced here: 401 us
  blocking collectives  265 us (66%)
  waiting for transfers between devices  85.6 us (21%)
  other arithmetic  19.3 us (5%)
  between operations  14.2 us (4%)
  matrix products  13.5 us (3%)
    psum x1, blocking collectives, body(): lax.psum(called_proj.astype(jnp.bfloat16), 'samp').astype(jnp.float32)  124 us
    unnamed x3, waiting for transfers between devices  68.9 us
    psum x1, blocking collectives, body(): lax.psum((jnp.sum(residual * residual, axis=0), jnp.sum(direction * appli...  66.8 us
    psum x1, blocking collectives, body(): lax.psum((res_square, jnp.sum(solution_new, axis=0), jnp.sum(solution_new...  63.2 us
    reduce_scatter x1, waiting for transfers between devices, body(): lax.psum_scatter((term / VARIANTS).astype(jnp.bfloat16), 'var', scatter_d...  16.6 us
    all_gather x1, blocking collectives, body(): piece = lax.all_gather(direction_b, 'var', axis=0, tiled=True)  11.4 us
    reduce_sum x1, other arithmetic, body(): allele_sum = jnp.sum(coded, axis=1).astype(jnp.float32)  10.1 us
  transfers between devices with their start and end apart: 2, of which 2 were waited for; matrix products, arithmetic and copies ran while one was open for 1% of the time, Pallas kernels for 0%

commit v1 on v0

v1 whole, which is shorter than its diff:
```python
import functools
import math

import jax
import jax.numpy as jnp
from jax import lax
from jax.experimental import pallas as pl
from jax.experimental.pallas import tpu as pltpu
from jax.sharding import PartitionSpec as P

VARIANTS = 3072
SAMPLES = 98304
IMPUTED = 1024
RHS = 16
NZ = 4
NP = 32
QUARTER = 768
WIDE = QUARTER * NZ
LOCAL = VARIANTS // NZ
BLK = 128
NBLK = LOCAL // BLK
F32 = jnp.float32
BF16 = jnp.bfloat16
MESH = pl.DeviceIdType.MESH


def owner_of(block, group):
    far = block + 10 - 4 * lax.rem(block // 2, 2)
    return 2 * (block + group * (far - block)) + group


def rows_iota(shape):
    return lax.broadcasted_iota(jnp.int32, shape, 0)


def lanes_iota(shape):
    return lax.broadcasted_iota(jnp.int32, shape, 1)


def to_column(row):
    eye = rows_iota((RHS, RHS)) == lanes_iota((RHS, RHS))
    return jnp.sum(jnp.where(eye, jnp.broadcast_to(row, (RHS, RHS)), 0.0), axis=1, keepdims=True)


def spread_columns(columns):
    rows, lanes = rows_iota((RHS, 128)), lanes_iota((RHS, 128))
    total = jnp.zeros((RHS, 128), F32)
    for k, column in enumerate(columns):
        total = jnp.where(lanes == rows + RHS * k, column, total)
    return total[:8] + total[8:]


def kernel(
    gen, cal, dos, order, noise, sol, res, dirn,
    sol_new, res_new, dir_new, scores,
    gv, cv, dv, xb, dx, db, hot, stat_s, stat_r, rs_s, rs_r, ag_s, ag_r, g_acc, g_s, g_r,
    q_acc, q_r, cz_s, cz_r, cp_s, cp_r, d1_s, d1_r, d2_s, d2_r,
    load_sem, a_send, a_recv, st_send, st_recv, rs_send, rs_recv, ag_send, ag_recv,
    g_send, g_recv, q_send, q_recv, cz_send, cz_recv, cp_send, cp_recv, d1_send, d1_recv, d2_send, d2_recv,
):
    z = lax.axis_index("var")
    me = lax.axis_index("samp")
    core = lax.rem(me, 2)
    chip = me // 2

    def z_peer(k):
        return {"var": lax.rem(z + k, NZ), "samp": me}

    def p_peer(k):
        return {"var": z, "samp": lax.rem(me + k, NP)}

    def d1_peer(k):
        return {"var": lax.rem(z + k // 2, NZ), "samp": 2 * chip + lax.rem(core + lax.rem(k, 2), 2)}

    def remote(src, dst, send, recv, device):
        return pltpu.make_async_remote_copy(
            src_ref=src, dst_ref=dst, send_sem=send, recv_sem=recv, device_id=device, device_id_type=MESH
        )

    def load(j, which):
        source, target = ((gen, gv), (cal, cv))[which]
        return pltpu.make_async_copy(
            source.at[pl.ds(pl.multiple_of(j * BLK, BLK), BLK), :], target.at[j], load_sem.at[which, j]
        )

    load_dos = pltpu.make_async_copy(dos, dv, load_sem.at[0, NBLK])

    for j in range(3):
        load(j, 0).start()
        load(j, 1).start()

    barrier = pltpu.get_barrier_semaphore()

    def greet_plane(k, carry):
        pl.semaphore_signal(barrier, inc=1, device_id=p_peer(k), device_id_type=MESH)
        return carry

    def greet_near(k, carry):
        pl.semaphore_signal(barrier, inc=1, device_id=d1_peer(k), device_id_type=MESH)
        return carry

    lax.fori_loop(1, NP, greet_plane, 0)
    lax.fori_loop(2, 8, greet_near, 0)

    d = dirn[...]
    r = res[...]
    d_b = d.astype(BF16)
    dx[:RHS, pl.ds(pl.multiple_of(z * QUARTER, QUARTER), QUARTER)] = d_b
    dx[RHS:, :] = jnp.ones((RHS, WIDE), BF16)
    r_col = jnp.sum(r * r, axis=1, keepdims=True)
    d_col = jnp.sum(d * d, axis=1, keepdims=True)
    pair = jnp.sum(spread_columns((r_col, d_col)), axis=0, keepdims=True)
    row8, lane8 = rows_iota((8, 128)), lanes_iota((8, 128))
    stat_s[...] = jnp.where(row8 == 2, pair, jnp.where(row8 == 3, pltpu.roll(jnp.broadcast_to(pair, (8, 128)), 112, 1), 0.0))
    g_acc[...] = jnp.zeros((RHS, WIDE), F32)
    q_acc[...] = jnp.zeros((8, 128), F32)

    pl.semaphore_wait(barrier, NP - 1 + 6)

    def direction_copy(k):
        mine = dx.at[pl.ds(0, RHS), pl.ds(pl.multiple_of(z * QUARTER, QUARTER), QUARTER)]
        return remote(mine, mine, a_send.at[k - 1], a_recv.at[k - 1], z_peer(k))

    def stat_copy(k):
        return remote(stat_s, stat_r.at[k - 1], st_send.at[k - 1], st_recv.at[k - 1], z_peer(k))

    for k in range(1, NZ):
        direction_copy(k).start()
        stat_copy(k).start()
    for k in range(1, NZ):
        stat_copy(k).wait()
    stats = stat_s[...] + stat_r[0] + stat_r[1] + stat_r[2]
    for k in range(1, NZ):
        direction_copy(k).wait()

    def rs_copy(j, group):
        owner = owner_of(j, group)
        slot = lax.rem(me - owner + NP - 1 + NP, NP)
        return remote(
            rs_s.at[j, group], rs_r.at[slot], rs_send.at[j, group], rs_recv, {"var": z, "samp": owner}
        )

    def chunk(j):
        load(j, 0).wait()
        load(j, 1).wait()

        @pl.when(j + 3 < NBLK)
        def _():
            load(j + 3, 0).start()
            load(j + 3, 1).start()

        @pl.when(j + 3 == NBLK)
        def _():
            load_dos.start()

        def convert(i, carry):
            first = pl.multiple_of(i * 16, 16)
            called = cv[j, pl.ds(first, 16), :].astype(F32).astype(BF16)
            codes = gv[j, pl.ds(first, 16), :].astype(F32).astype(BF16)
            xb[j, pl.ds(first, 16), :] = codes * called
            xb[j, pl.ds(pl.multiple_of(first + BLK, 16), 16), :] = called
            return carry

        lax.fori_loop(0, BLK // 16, convert, 0)
        proj = lax.dot_general(dx[...], xb[j], (((1,), (1,)), ((), ())), preferred_element_type=F32)
        counts = jnp.where(row8 == 0, proj[16:24, :BLK], jnp.where(row8 == 1, proj[16:24, BLK:], stats))
        for group in range(2):
            rs_s[j, group, 0:8, :] = proj[8 * group:8 * group + 8, :BLK]
            rs_s[j, group, 8:16, :] = proj[8 * group:8 * group + 8, BLK:]
            rs_s[j, group, 16:24, :] = counts

            @pl.when(me != owner_of(j, group))
            def _():
                rs_copy(j, group).start()

    def ag_copy(j, group, k):
        return remote(ag_r.at[j, group], ag_r.at[j, group], ag_send, ag_recv.at[j, group], p_peer(k))

    def owner_part(j):
        first, second = owner_of(j, 0), owner_of(j, 1)

        @pl.when((me == first) | (me == second))
        def _():
            group = (me == second).astype(jnp.int32)
            pltpu.make_async_copy(rs_r, rs_r, rs_recv).wait()
            total = rs_s[j, group] + jnp.sum(rs_r[...], axis=0)
            raw, called = total[0:8], total[8:16]
            frequency = (total[16:17] + 1.0) / (2.0 * total[17:18] + 2.0)
            spread = jnp.sqrt(2.0 * frequency * (1.0 - frequency))
            loading = (raw - 2.0 * frequency * called) / spread
            scaled_a = loading / spread
            scaled_b = 2.0 * frequency * loading / spread
            square = jnp.sum(loading * loading, axis=1, keepdims=True)
            square = jnp.sum(jnp.where(lane8 == row8 + 8 * group, square, 0.0), axis=0, keepdims=True)
            tail = jnp.where(row8 == 0, square, jnp.where((row8 == 2) | (row8 == 3), total[16:24], 0.0))
            high = tail.astype(BF16).astype(F32)
            ag_r[j, group] = jnp.concatenate([scaled_a, -scaled_b, high, tail - high], axis=0).astype(BF16)

            def send(k, carry):
                ag_copy(j, group, k).start()
                return carry

            lax.fori_loop(1, NP, send, 0)

    def back(j):
        halves = []
        for group in range(2):
            @pl.when(me != owner_of(j, group))
            def _():
                ag_copy(j, group, 1).wait_recv()

            halves.append(ag_r[j, group].astype(F32))
        left = jnp.concatenate([half[0:8] for half in halves], axis=0)
        right = jnp.concatenate([half[8:16] for half in halves], axis=0)
        weights = jnp.concatenate([left, right], axis=1).astype(BF16)
        q_acc[...] += (halves[0][16:24] + halves[0][24:32]) + (halves[1][16:24] + halves[1][24:32])
        return weights

    def back_product(j, weights):
        g_acc[...] += jnp.dot(weights, xb[j], preferred_element_type=F32)

    def step(j, carry):
        chunk(j)

        @pl.when(j >= 2)
        def _():
            owner_part(j - 2)

        @pl.when(j >= 4)
        def _():
            back_product(j - 4, back(j - 4))

        return carry

    lax.fori_loop(0, NBLK, step, 0)
    owner_part(NBLK - 2)

    load_dos.wait()

    def one_hot(i, carry):
        first = pl.multiple_of(i * 16, 16)
        hot[pl.ds(first, 16), :] = jnp.where(rows_iota((16, QUARTER)) + first == order[...], 1.0, 0.0).astype(BF16)
        return carry

    lax.fori_loop(0, QUARTER // 16, one_hot, 0)

    def convert_dose(i, carry):
        first = pl.multiple_of(i * 16, 16)
        db[pl.ds(first, 16), :] = dv[pl.ds(first, 16), :].astype(F32).astype(BF16)
        return carry

    lax.fori_loop(0, QUARTER // 16, convert_dose, 0)
    s = sol[...]
    s_high = s.astype(BF16)
    s_low = (s - s_high.astype(F32)).astype(BF16)
    d_low = (d - d_b.astype(F32)).astype(BF16)
    parts = jnp.concatenate([s_high, s_low, d_b, d_low], axis=0)
    picked = jnp.dot(parts, hot[...], preferred_element_type=F32).astype(BF16)
    picked = jnp.concatenate([picked, jnp.ones((RHS, QUARTER), BF16)], axis=0)
    cross = jnp.dot(picked, db[...], preferred_element_type=F32)
    cz_s[0:16, :] = cross[0:16] + cross[16:32]
    cz_s[16:32, :] = cross[32:48] + cross[48:64]
    cz_s[32:40, :] = cross[64:72]
    part = IMPUTED // NZ

    def cz_copy(k):
        peer = lax.rem(z + k, NZ)
        return remote(
            cz_s.at[:, pl.ds(pl.multiple_of(peer * part, part), part)], cz_r.at[k - 1],
            cz_send.at[k - 1], cz_recv.at[k - 1], z_peer(k),
        )

    for k in range(1, NZ):
        cz_copy(k).start()

    owner_part(NBLK - 1)
    for j in range(2, NBLK - 1):
        back_product(j, back(j))

    for k in range(1, NZ):
        cz_copy(k).wait()
    own = cz_s[:, pl.ds(pl.multiple_of(z * part, part), part)] + cz_r[0] + cz_r[1] + cz_r[2]
    own = jnp.concatenate([own, jnp.zeros((128 - 40, part), F32)], axis=0)
    cp_s[...] = jnp.transpose(own).reshape(NP, 8, 128)

    def cp_copy(k):
        return remote(cp_s.at[lax.rem(me + k, NP)], cp_r.at[k - 1], cp_send, cp_recv, p_peer(k))

    def send_cp(k, carry):
        cp_copy(k).start()
        return carry

    weights = back(NBLK - 1)

    def q_copy(k):
        return remote(q_acc, q_r.at[k - 1], q_send.at[k - 1], q_recv.at[k - 1], z_peer(k))

    for k in range(1, NZ):
        q_copy(k).start()
    back_product(NBLK - 1, weights)
    g_s[...] = (g_acc[...] * (1.0 / VARIANTS)).astype(BF16)

    def g_copy(k):
        peer = lax.rem(z + k, NZ)
        return remote(
            g_s.at[:, pl.ds(pl.multiple_of(peer * QUARTER, QUARTER), QUARTER)], g_r.at[k - 1],
            g_send.at[k - 1], g_recv.at[k - 1], z_peer(k),
        )

    for k in range(1, NZ):
        g_copy(k).start()
    lax.fori_loop(1, NP, send_cp, 0)

    for k in range(1, NZ):
        q_copy(k).wait()
    q = q_acc[...]
    square = (q[0:1] + q_r[0, 0:1] + q_r[1, 0:1] + q_r[2, 0:1])[:, :RHS]
    res_norm = q[2:3, :RHS] * (1.0 / (2 * NBLK))
    dir_norm = q[3:4, :RHS] * (1.0 / (2 * NBLK))
    curvature = noise[...] * dir_norm + square * (1.0 / VARIANTS)
    step_row = res_norm / (curvature + 1e-6)
    step_col = to_column(step_row)
    s_next = s + step_col * d
    sol_new[...] = s_next
    s_sum = jnp.sum(s_next, axis=1, keepdims=True)
    s_square = jnp.sum(s_next * s_next, axis=1, keepdims=True)
    own_g = g_acc[:, pl.ds(pl.multiple_of(z * QUARTER, QUARTER), QUARTER)] * (1.0 / VARIANTS)
    base = to_column(noise[...]) * d + own_g
    for k in range(1, NZ):
        g_copy(k).wait()
    applied = base + g_r[0].astype(F32) + g_r[1].astype(F32) + g_r[2].astype(F32)
    r_next = r - step_col * applied
    res_new[...] = r_next
    r_square = jnp.sum(r_next * r_next, axis=1, keepdims=True)
    d1_s[...] = spread_columns((r_square, s_sum, s_square))

    def d1_copy(k):
        return remote(d1_s, d1_r.at[k - 1], d1_send.at[k - 1], d1_recv.at[k - 1], d1_peer(k))

    for k in range(1, 8):
        d1_copy(k).start()
    pltpu.make_async_copy(cp_r, cp_r, cp_recv).wait()
    dose = cp_s[me] + jnp.sum(cp_r[...], axis=0)
    for k in range(1, 8):
        d1_copy(k).wait()
    d2_s[...] = d1_s[...] + jnp.sum(d1_r[...], axis=0)

    def d2_copy(k):
        return remote(
            d2_s, d2_r.at[k - 1], d2_send, d2_recv, {"var": z, "samp": lax.rem(me + 2 * k, NP)}
        )

    def send_d2(k, carry):
        d2_copy(k).start()
        return carry

    lax.fori_loop(1, NP // 2, send_d2, 0)
    dose_freq = (dose[:, 32:33] * (1.0 / 100.0) + 1.0) / (2.0 * SAMPLES + 2.0)
    dose_spread = jnp.sqrt(2.0 * dose_freq * (1.0 - dose_freq))
    cross_sum = dose[:, 0:RHS] + step_row * dose[:, RHS:2 * RHS]
    pltpu.make_async_copy(d2_r, d2_r, d2_recv).wait()
    sums = jnp.sum(d2_s[...] + jnp.sum(d2_r[...], axis=0), axis=0, keepdims=True)
    beta = to_column(sums[:, 0:RHS] / (res_norm + 1e-6))
    dir_new[...] = r_next + beta * d
    scale = math.sqrt(SAMPLES) * jnp.sqrt(sums[:, 2 * RHS:3 * RHS] * (1.0 / SAMPLES) + 1e-6)
    scores[...] = (cross_sum * (1.0 / 100.0) - 2.0 * dose_freq * sums[:, RHS:2 * RHS]) / (dose_spread * scale)

    pltpu.make_async_copy(d2_r, d2_r, d2_send).wait()
    pltpu.make_async_copy(cp_r, cp_r, cp_send).wait()

    def sent(j, carry):
        for group in range(2):
            @pl.when(me != owner_of(j, group))
            def _():
                rs_copy(j, group).wait_send()

            @pl.when(me == owner_of(j, group))
            def _():
                view = rs_r.at[:, pl.ds(0, 16), :]
                pltpu.make_async_copy(view, view, ag_send).wait()

        return carry

    lax.fori_loop(0, NBLK, sent, 0)


def body(genotypes, called, dosage, sample_order, noise_ratio, solution, residual, direction):
    vmem = pl.BlockSpec(memory_space=pltpu.VMEM)
    hbm = pl.BlockSpec(memory_space=pl.ANY)
    dma = pltpu.SemaphoreType.DMA
    small = jax.ShapeDtypeStruct((RHS, QUARTER), F32)
    outs = pl.pallas_call(
        kernel,
        out_shape=(small, small, small, jax.ShapeDtypeStruct((8, RHS), F32)),
        in_specs=[hbm] * 3 + [vmem] * 5,
        out_specs=(vmem,) * 4,
        scratch_shapes=[
            pltpu.VMEM((NBLK, BLK, WIDE), jnp.int32),
            pltpu.VMEM((NBLK, BLK, WIDE), jnp.int32),
            pltpu.VMEM((QUARTER, IMPUTED), jnp.int32),
            pltpu.VMEM((NBLK, 2 * BLK, WIDE), BF16),
            pltpu.VMEM((2 * RHS, WIDE), BF16),
            pltpu.VMEM((QUARTER, IMPUTED), BF16),
            pltpu.VMEM((QUARTER, QUARTER), BF16),
            pltpu.VMEM((8, 128), F32),
            pltpu.VMEM((NZ - 1, 8, 128), F32),
            pltpu.VMEM((NBLK, 2, 24, 128), F32),
            pltpu.VMEM((NP - 1, 24, 128), F32),
            pltpu.VMEM((8, 128), F32),
            pltpu.VMEM((NBLK, 2, 32, 128), BF16),
            pltpu.VMEM((RHS, WIDE), F32),
            pltpu.VMEM((RHS, WIDE), BF16),
            pltpu.VMEM((NZ - 1, RHS, QUARTER), BF16),
            pltpu.VMEM((8, 128), F32),
            pltpu.VMEM((NZ - 1, 8, 128), F32),
            pltpu.VMEM((40, IMPUTED), F32),
            pltpu.VMEM((NZ - 1, 40, IMPUTED // NZ), F32),
            pltpu.VMEM((NP, 8, 128), F32),
            pltpu.VMEM((NP - 1, 8, 128), F32),
            pltpu.VMEM((8, 128), F32),
            pltpu.VMEM((7, 8, 128), F32),
            pltpu.VMEM((8, 128), F32),
            pltpu.VMEM((NP // 2 - 1, 8, 128), F32),
            dma((2, NBLK + 1)),
            dma((3,)), dma((3,)),
            dma((3,)), dma((3,)),
            dma((NBLK, 2)), dma,
            dma, dma((NBLK, 2)),
            dma((3,)), dma((3,)),
            dma((3,)), dma((3,)),
            dma((3,)), dma((3,)),
            dma, dma,
            dma((7,)), dma((7,)),
            dma, dma,
        ],
        compiler_params=pltpu.CompilerParams(
            collective_id=0, has_side_effects=True, vmem_limit_bytes=56 * 1024 * 1024
        ),
        cost_estimate=pl.CostEstimate(flops=400_000_000, bytes_accessed=22_000_000, transcendentals=0),
        name="cg_step",
    )(
        genotypes, called, dosage, sample_order, noise_ratio.reshape(1, RHS),
        solution.T, residual.T, direction.T,
    )
    sol_new, res_new, dir_new, scores = outs
    return (sol_new.T, res_new.T, dir_new.T, scores)


def solution(mesh):
    rows = P(("samp", "var"), None)
    return jax.shard_map(
        body,
        mesh=mesh,
        in_specs=(P("var", "samp"), P("var", "samp"), rows, rows, P(), rows, rows, rows),
        out_specs=(rows, rows, rows, P(("var", "samp"), None)),
        check_vma=False,
    )
```

time: 402 us -> 55.3 us (0.14)
  blocking collectives: 265 us -> 0 us
  waiting for transfers between devices: 85.6 us -> 0 us
  Pallas kernels: 0 us -> 48.7 us
  other arithmetic: 19.3 us -> 0 us
  between operations: 14.2 us -> 0.64 us
  matrix products: 13.5 us -> 0 us
    psum x3 -> x0, blocking collectives: 254 us -> none  [the longest x1 124 us: body(): lax.psum(called_proj.astype(jnp.bfloat16), 'samp').astype(jnp.float32)]
    unnamed x3 -> x0, waiting for transfers between devices: 68.9 us -> none
    pallas_call x0 -> x1, Pallas kernels: none -> 48.7 us  [body(): pl.pallas_call(kernel, out_shape=(small, small, small, jax.ShapeDtypeStru...]
    reduce_scatter x1 -> x0, waiting for transfers between devices: 16.6 us -> none  [body(): lax.psum_scatter((term / VARIANTS).astype(jnp.bfloat16), 'var', scatter_d...]
    reduce_sum x5 -> x0, other arithmetic: 15.5 us -> none  [the longest x1 10.1 us: body(): allele_sum = jnp.sum(coded, axis=1).astype(jnp.float32)]
    dot_general x5 -> x0, matrix products: 13.5 us -> none  [the longest x1 5.15 us: body(): jnp.dot(called_cols, piece, preferred_element_type=jnp.float32)]
    all_gather x1 -> x0, blocking collectives: 11.4 us -> none  [body(): piece = lax.all_gather(direction_b, 'var', axis=0, tiled=True)]
  transfers between devices with their start and end apart: 2 -> 0, of which waited for: 2 -> 0; matrix products, arithmetic and copies ran while one was open for 1% -> 0% of each run, Pallas kernels for 0% -> 0%
where the time goes in v1:
time: 55.3 us; the launch traced here: 54.9 us
  Pallas kernels  48.7 us (88%)
  local copies, waits for them, and re-layouts  5.53 us (10%)
  between operations  0.64 us (1%)
    pallas_call x1, Pallas kernels, body(): pl.pallas_call(kernel, out_shape=(small, small, small, jax.ShapeDtypeStru...  48.7 us
    unnamed x4, local copies, waits for them, and re-layouts  5.53 us

profile of v1, /device:TPU:1, one launch (start us, length us, event | category | flops | bytes accessed | tf_op | source)
XLA Modules:
  0.0 54.9 jit_solution(10568469138683757438)
XLA Ops:
  0.6 48.7 %cg_step.1 = (f32[16,768]{1,0:T(8,128)}, f32[16,768]{1,0:T(8,128)}, f32[16,768]{1,0:T(8,128)}, f32[8,16]{1,0:T(8,128)}) custom-call(s32[768,3072]{1,0:T(8,128)} %gen.1, s32[768,3072]{1,0:T(8,128)} %cal.1, s32[768,1024]{1,0:T(8,128)} %dos.1, s32[1,768]{1,0:T(1,128)} %order.1, f32[1,16]{1,0:T(1,128)} %bitcast.13, f32[16,768]{1,0:T(8,128)} %bitcast.10, ...), custom_call_target="tpu_custom_call" | custom-call | flops 400000000 | bytes 22000000 | tf_op jit(solution)/shard_map/cg_step/pallas_call | solution.py:392
  49.4 1.4 %copy.16 = f32[768,16]{0,1:T(8,128)} copy(f32[768,16]{0,1:T(8,128)} %bitcast.9) | data formatting | bytes 98304
  50.8 1.4 %copy.17 = f32[768,16]{0,1:T(8,128)} copy(f32[768,16]{0,1:T(8,128)} %bitcast.8) | data formatting | bytes 98304
  52.2 1.4 %copy.18 = f32[768,16]{0,1:T(8,128)} copy(f32[768,16]{0,1:T(8,128)} %bitcast.7) | data formatting | bytes 98304
  53.6 1.3 %copy.19 = f32[8,16]{1,0:T(8,128)} copy(f32[8,16]{1,0:T(8,128)} %get-tuple-element.19) | data formatting | bytes 1024

commit v2 on v1

--- a/solution.py
+++ b/solution.py
@@ -1,4 +1,3 @@
-import functools
 import math
 
 import jax
@@ -19,6 +18,8 @@
 LOCAL = VARIANTS // NZ
 BLK = 128
 NBLK = LOCAL // BLK
+WINDOW = 3
+EARLY = 3
 F32 = jnp.float32
 BF16 = jnp.bfloat16
 MESH = pl.DeviceIdType.MESH
@@ -51,17 +52,16 @@
 
 
 def kernel(
-    gen, cal, dos, order, noise, sol, res, dirn,
+    gen, cal, dos, order_in, noise_in, sol_in, res_in, dir_in,
     sol_new, res_new, dir_new, scores,
-    gv, cv, dv, xb, dx, db, hot, stat_s, stat_r, rs_s, rs_r, ag_s, ag_r, g_acc, g_s, g_r,
+    order, noise, sol, res, dirn, gv, cv, dv, xb, dx, db, hot, stat_s, stat_r, rs_s, rs_r, ag_r, sq_r, g_acc, g_s, g_r,
     q_acc, q_r, cz_s, cz_r, cp_s, cp_r, d1_s, d1_r, d2_s, d2_r,
-    load_sem, a_send, a_recv, st_send, st_recv, rs_send, rs_recv, ag_send, ag_recv,
+    in_sem, load_sem, a_send, a_recv, st_send, st_recv, rs_send, rs_recv, ag_send, ag_recv,
+    sq_send, sq_recv,
     g_send, g_recv, q_send, q_recv, cz_send, cz_recv, cp_send, cp_recv, d1_send, d1_recv, d2_send, d2_recv,
 ):
     z = lax.axis_index("var")
     me = lax.axis_index("samp")
-    core = lax.rem(me, 2)
-    chip = me // 2
 
     def z_peer(k):
         return {"var": lax.rem(z + k, NZ), "samp": me}
@@ -69,8 +69,12 @@
     def p_peer(k):
         return {"var": z, "samp": lax.rem(me + k, NP)}
 
-    def d1_peer(k):
-        return {"var": lax.rem(z + k // 2, NZ), "samp": 2 * chip + lax.rem(core + lax.rem(k, 2), 2)}
+    def each_block(first, last, work):
+        lax.fori_loop(first, last, lambda j, carry: (work(j), carry)[1], 0)
+
+    def each_plane_peer(send):
+        for first in (16, 8, 24, 0):
+            lax.fori_loop(max(first, 1), first + 8, lambda k, carry: (send(k), carry)[1], 0)
 
     def remote(src, dst, send, recv, device):
         return pltpu.make_async_remote_copy(
@@ -85,22 +89,28 @@
 
     load_dos = pltpu.make_async_copy(dos, dv, load_sem.at[0, NBLK])
 
-    for j in range(3):
+    smalls = [
+        pltpu.make_async_copy(source, target, in_sem.at[i])
+        for i, (source, target) in enumerate(
+            ((dir_in, dirn), (res_in, res), (sol_in, sol), (noise_in, noise), (order_in, order))
+        )
+    ]
+    for copy in smalls:
+        copy.start()
+    for j in range(WINDOW):
         load(j, 0).start()
         load(j, 1).start()
 
     barrier = pltpu.get_barrier_semaphore()
 
-    def greet_plane(k, carry):
-        pl.semaphore_signal(barrier, inc=1, device_id=p_peer(k), device_id_type=MESH)
-        return carry
-
-    def greet_near(k, carry):
-        pl.semaphore_signal(barrier, inc=1, device_id=d1_peer(k), device_id_type=MESH)
-        return carry
-
-    lax.fori_loop(1, NP, greet_plane, 0)
-    lax.fori_loop(2, 8, greet_near, 0)
+    def greet(device):
+        pl.semaphore_signal(barrier, inc=1, device_id=device, device_id_type=MESH)
+
+    for k in range(1, NZ):
+        greet(z_peer(k))
+    each_plane_peer(lambda k: greet(p_peer(k)))
+    for copy in smalls:
+        copy.wait()
 
     d = dirn[...]
     r = res[...]
@@ -109,13 +119,12 @@
     dx[RHS:, :] = jnp.ones((RHS, WIDE), BF16)
     r_col = jnp.sum(r * r, axis=1, keepdims=True)
     d_col = jnp.sum(d * d, axis=1, keepdims=True)
-    pair = jnp.sum(spread_columns((r_col, d_col)), axis=0, keepdims=True)
     row8, lane8 = rows_iota((8, 128)), lanes_iota((8, 128))
-    stat_s[...] = jnp.where(row8 == 2, pair, jnp.where(row8 == 3, pltpu.roll(jnp.broadcast_to(pair, (8, 128)), 112, 1), 0.0))
+    pair = jnp.sum(spread_columns((jnp.zeros_like(r_col), r_col, d_col)), axis=0, keepdims=True)
+    stat_s[...] = jnp.where(row8 == 2, pair, 0.0)
     g_acc[...] = jnp.zeros((RHS, WIDE), F32)
-    q_acc[...] = jnp.zeros((8, 128), F32)
-
-    pl.semaphore_wait(barrier, NP - 1 + 6)
+
+    pl.semaphore_wait(barrier, NP - 1 + NZ - 1)
 
     def direction_copy(k):
         mine = dx.at[pl.ds(0, RHS), pl.ds(pl.multiple_of(z * QUARTER, QUARTER), QUARTER)]
@@ -127,12 +136,6 @@
     for k in range(1, NZ):
         direction_copy(k).start()
         stat_copy(k).start()
-    for k in range(1, NZ):
-        stat_copy(k).wait()
-    stats = stat_s[...] + stat_r[0] + stat_r[1] + stat_r[2]
-    for k in range(1, NZ):
-        direction_copy(k).wait()
-
     def rs_copy(j, group):
         owner = owner_of(j, group)
         slot = lax.rem(me - owner + NP - 1 + NP, NP)
@@ -140,16 +143,16 @@
             rs_s.at[j, group], rs_r.at[slot], rs_send.at[j, group], rs_recv, {"var": z, "samp": owner}
         )
 
-    def chunk(j):
+    def convert_block(j):
         load(j, 0).wait()
         load(j, 1).wait()
 
-        @pl.when(j + 3 < NBLK)
+        @pl.when(j + WINDOW < NBLK)
         def _():
-            load(j + 3, 0).start()
-            load(j + 3, 1).start()
-
-        @pl.when(j + 3 == NBLK)
+            load(j + WINDOW, 0).start()
+            load(j + WINDOW, 1).start()
+
+        @pl.when(j + WINDOW == NBLK)
         def _():
             load_dos.start()
 
@@ -162,6 +165,8 @@
             return carry
 
         lax.fori_loop(0, BLK // 16, convert, 0)
+
+    def project_block(j, stats):
         proj = lax.dot_general(dx[...], xb[j], (((1,), (1,)), ((), ())), preferred_element_type=F32)
         counts = jnp.where(row8 == 0, proj[16:24, :BLK], jnp.where(row8 == 1, proj[16:24, BLK:], stats))
         for group in range(2):
@@ -175,6 +180,9 @@
 
     def ag_copy(j, group, k):
         return remote(ag_r.at[j, group], ag_r.at[j, group], ag_send, ag_recv.at[j, group], p_peer(k))
+
+    def sq_copy(j, group, k):
+        return remote(sq_r.at[j, group], sq_r.at[j, group], sq_send, sq_recv.at[j, group], p_peer(k))
 
     def owner_part(j):
         first, second = owner_of(j, 0), owner_of(j, 1)
@@ -190,17 +198,12 @@
             loading = (raw - 2.0 * frequency * called) / spread
             scaled_a = loading / spread
             scaled_b = 2.0 * frequency * loading / spread
+            ag_r[j, group] = jnp.concatenate([scaled_a, -scaled_b], axis=0).astype(BF16)
+            each_plane_peer(lambda k: ag_copy(j, group, k).start())
             square = jnp.sum(loading * loading, axis=1, keepdims=True)
             square = jnp.sum(jnp.where(lane8 == row8 + 8 * group, square, 0.0), axis=0, keepdims=True)
-            tail = jnp.where(row8 == 0, square, jnp.where((row8 == 2) | (row8 == 3), total[16:24], 0.0))
-            high = tail.astype(BF16).astype(F32)
-            ag_r[j, group] = jnp.concatenate([scaled_a, -scaled_b, high, tail - high], axis=0).astype(BF16)
-
-            def send(k, carry):
-                ag_copy(j, group, k).start()
-                return carry
-
-            lax.fori_loop(1, NP, send, 0)
+            sq_r[j, group] = square + jnp.where(lane8[:1] >= RHS, total[18:19], 0.0)
+            each_plane_peer(lambda k: sq_copy(j, group, k).start())
 
     def back(j):
         halves = []
@@ -213,27 +216,25 @@
         left = jnp.concatenate([half[0:8] for half in halves], axis=0)
         right = jnp.concatenate([half[8:16] for half in halves], axis=0)
         weights = jnp.concatenate([left, right], axis=1).astype(BF16)
-        q_acc[...] += (halves[0][16:24] + halves[0][24:32]) + (halves[1][16:24] + halves[1][24:32])
         return weights
 
     def back_product(j, weights):
         g_acc[...] += jnp.dot(weights, xb[j], preferred_element_type=F32)
 
-    def step(j, carry):
-        chunk(j)
-
-        @pl.when(j >= 2)
-        def _():
-            owner_part(j - 2)
-
-        @pl.when(j >= 4)
-        def _():
-            back_product(j - 4, back(j - 4))
-
-        return carry
-
-    lax.fori_loop(0, NBLK, step, 0)
-    owner_part(NBLK - 2)
+    each_block(0, EARLY, convert_block)
+    for k in range(1, NZ):
+        stat_copy(k).wait()
+    stats = stat_s[...] + stat_r[0] + stat_r[1] + stat_r[2]
+    for k in range(1, NZ):
+        direction_copy(k).wait()
+    each_block(0, EARLY, lambda j: project_block(j, stats))
+
+    def convert_and_project(j):
+        convert_block(j)
+        project_block(j, stats)
+
+    each_block(EARLY, NBLK, convert_and_project)
+    each_block(0, NBLK - 2, owner_part)
 
     load_dos.wait()
 
@@ -273,9 +274,8 @@
     for k in range(1, NZ):
         cz_copy(k).start()
 
-    owner_part(NBLK - 1)
-    for j in range(2, NBLK - 1):
-        back_product(j, back(j))
+    each_block(NBLK - 2, NBLK, owner_part)
+    each_block(0, NBLK - 1, lambda j: back_product(j, back(j)))
 
     for k in range(1, NZ):
         cz_copy(k).wait()
@@ -286,11 +286,16 @@
     def cp_copy(k):
         return remote(cp_s.at[lax.rem(me + k, NP)], cp_r.at[k - 1], cp_send, cp_recv, p_peer(k))
 
-    def send_cp(k, carry):
-        cp_copy(k).start()
-        return carry
-
+    each_plane_peer(lambda k: cp_copy(k).start())
     weights = back(NBLK - 1)
+
+    for j in range(NBLK):
+        for group in range(2):
+            @pl.when(me != owner_of(j, group))
+            def _():
+                sq_copy(j, group, 1).wait_recv()
+
+    q_acc[...] = jnp.sum(sq_r[...], axis=(0, 1))
 
     def q_copy(k):
         return remote(q_acc, q_r.at[k - 1], q_send.at[k - 1], q_recv.at[k - 1], z_peer(k))
@@ -309,14 +314,13 @@
 
     for k in range(1, NZ):
         g_copy(k).start()
-    lax.fori_loop(1, NP, send_cp, 0)
 
     for k in range(1, NZ):
         q_copy(k).wait()
     q = q_acc[...]
-    square = (q[0:1] + q_r[0, 0:1] + q_r[1, 0:1] + q_r[2, 0:1])[:, :RHS]
-    res_norm = q[2:3, :RHS] * (1.0 / (2 * NBLK))
-    dir_norm = q[3:4, :RHS] * (1.0 / (2 * NBLK))
+    square = (q + q_r[0] + q_r[1] + q_r[2])[:, :RHS]
+    res_norm = q[:, RHS:2 * RHS] * (1.0 / (2 * NBLK))
+    dir_norm = q[:, 2 * RHS:3 * RHS] * (1.0 / (2 * NBLK))
     curvature = noise[...] * dir_norm + square * (1.0 / VARIANTS)
     step_row = res_norm / (curvature + 1e-6)
     step_col = to_column(step_row)
@@ -335,31 +339,25 @@
     d1_s[...] = spread_columns((r_square, s_sum, s_square))
 
     def d1_copy(k):
-        return remote(d1_s, d1_r.at[k - 1], d1_send.at[k - 1], d1_recv.at[k - 1], d1_peer(k))
-
-    for k in range(1, 8):
+        return remote(d1_s, d1_r.at[k - 1], d1_send.at[k - 1], d1_recv.at[k - 1], z_peer(k))
+
+    for k in range(1, NZ):
         d1_copy(k).start()
     pltpu.make_async_copy(cp_r, cp_r, cp_recv).wait()
     dose = cp_s[me] + jnp.sum(cp_r[...], axis=0)
-    for k in range(1, 8):
+    for k in range(1, NZ):
         d1_copy(k).wait()
-    d2_s[...] = d1_s[...] + jnp.sum(d1_r[...], axis=0)
+    d2_s[...] = jnp.sum(d1_s[...] + jnp.sum(d1_r[...], axis=0), axis=0, keepdims=True)
 
     def d2_copy(k):
-        return remote(
-            d2_s, d2_r.at[k - 1], d2_send, d2_recv, {"var": z, "samp": lax.rem(me + 2 * k, NP)}
-        )
-
-    def send_d2(k, carry):
-        d2_copy(k).start()
-        return carry
-
-    lax.fori_loop(1, NP // 2, send_d2, 0)
+        return remote(d2_s, d2_r.at[k - 1], d2_send, d2_recv, p_peer(k))
+
+    each_plane_peer(lambda k: d2_copy(k).start())
     dose_freq = (dose[:, 32:33] * (1.0 / 100.0) + 1.0) / (2.0 * SAMPLES + 2.0)
     dose_spread = jnp.sqrt(2.0 * dose_freq * (1.0 - dose_freq))
     cross_sum = dose[:, 0:RHS] + step_row * dose[:, RHS:2 * RHS]
     pltpu.make_async_copy(d2_r, d2_r, d2_recv).wait()
-    sums = jnp.sum(d2_s[...] + jnp.sum(d2_r[...], axis=0), axis=0, keepdims=True)
+    sums = d2_s[...] + jnp.sum(d2_r[...], axis=0)
     beta = to_column(sums[:, 0:RHS] / (res_norm + 1e-6))
     dir_new[...] = r_next + beta * d
     scale = math.sqrt(SAMPLES) * jnp.sqrt(sums[:, 2 * RHS:3 * RHS] * (1.0 / SAMPLES) + 1e-6)
@@ -376,8 +374,9 @@
 
             @pl.when(me == owner_of(j, group))
             def _():
-                view = rs_r.at[:, pl.ds(0, 16), :]
+                view = rs_r.at[:, pl.ds(0, 8), :]
                 pltpu.make_async_copy(view, view, ag_send).wait()
+                pltpu.make_async_copy(d2_r, d2_r, sq_send).wait()
 
         return carry
 
@@ -386,15 +385,20 @@
 
 def body(genotypes, called, dosage, sample_order, noise_ratio, solution, residual, direction):
     vmem = pl.BlockSpec(memory_space=pltpu.VMEM)
-    hbm = pl.BlockSpec(memory_space=pl.ANY)
+    hbm = pl.BlockSpec(memory_space=pltpu.HBM)
     dma = pltpu.SemaphoreType.DMA
     small = jax.ShapeDtypeStruct((RHS, QUARTER), F32)
     outs = pl.pallas_call(
         kernel,
-        out_shape=(small, small, small, jax.ShapeDtypeStruct((8, RHS), F32)),
-        in_specs=[hbm] * 3 + [vmem] * 5,
+        out_shape=(pltpu.VMEM((RHS, QUARTER), F32),) * 3 + (pltpu.VMEM((8, RHS), F32),),
+        in_specs=[hbm] * 8,
         out_specs=(vmem,) * 4,
         scratch_shapes=[
+            pltpu.VMEM((1, QUARTER), jnp.int32),
+            pltpu.VMEM((1, RHS), F32),
+            pltpu.VMEM((RHS, QUARTER), F32),
+            pltpu.VMEM((RHS, QUARTER), F32),
+            pltpu.VMEM((RHS, QUARTER), F32),
             pltpu.VMEM((NBLK, BLK, WIDE), jnp.int32),
             pltpu.VMEM((NBLK, BLK, WIDE), jnp.int32),
             pltpu.VMEM((QUARTER, IMPUTED), jnp.int32),
@@ -406,31 +410,33 @@
             pltpu.VMEM((NZ - 1, 8, 128), F32),
             pltpu.VMEM((NBLK, 2, 24, 128), F32),
             pltpu.VMEM((NP - 1, 24, 128), F32),
-            pltpu.VMEM((8, 128), F32),
-            pltpu.VMEM((NBLK, 2, 32, 128), BF16),
+            pltpu.VMEM((NBLK, 2, 16, 128), BF16),
+            pltpu.VMEM((NBLK, 2, 1, 128), F32),
             pltpu.VMEM((RHS, WIDE), F32),
             pltpu.VMEM((RHS, WIDE), BF16),
             pltpu.VMEM((NZ - 1, RHS, QUARTER), BF16),
-            pltpu.VMEM((8, 128), F32),
-            pltpu.VMEM((NZ - 1, 8, 128), F32),
+            pltpu.VMEM((1, 128), F32),
+            pltpu.VMEM((NZ - 1, 1, 128), F32),
             pltpu.VMEM((40, IMPUTED), F32),
             pltpu.VMEM((NZ - 1, 40, IMPUTED // NZ), F32),
             pltpu.VMEM((NP, 8, 128), F32),
             pltpu.VMEM((NP - 1, 8, 128), F32),
             pltpu.VMEM((8, 128), F32),
-            pltpu.VMEM((7, 8, 128), F32),
-            pltpu.VMEM((8, 128), F32),
-            pltpu.VMEM((NP // 2 - 1, 8, 128), F32),
+            pltpu.VMEM((NZ - 1, 8, 128), F32),
+            pltpu.VMEM((1, 128), F32),
+            pltpu.VMEM((NP - 1, 1, 128), F32),
+            dma((5,)),
             dma((2, NBLK + 1)),
             dma((3,)), dma((3,)),
             dma((3,)), dma((3,)),
             dma((NBLK, 2)), dma,
             dma, dma((NBLK, 2)),
+            dma, dma((NBLK, 2)),
             dma((3,)), dma((3,)),
             dma((3,)), dma((3,)),
             dma((3,)), dma((3,)),
             dma, dma,
-            dma((7,)), dma((7,)),
+            dma((3,)), dma((3,)),
             dma, dma,
         ],
         compiler_params=pltpu.CompilerParams(

time: 55.3 us -> 43.6 us (0.79)
  Pallas kernels: 48.7 us -> 40.4 us
  local copies, waits for them, and re-layouts: 5.53 us -> 2.45 us
    pallas_call x1, Pallas kernels: 48.7 us -> 40.4 us  [body(): pl.pallas_call(kernel, out_shape=(pltpu.VMEM((RHS, QUARTER), F32),) * 3 +...]
    unnamed x4, local copies, waits for them, and re-layouts: 5.53 us -> 2.45 us
where the time goes in v2:
time: 43.6 us; the launch traced here: 43.5 us
  Pallas kernels  40.4 us (93%)
  local copies, waits for them, and re-layouts  2.45 us (6%)
  between operations  0.64 us (1%)
    pallas_call x1, Pallas kernels, body(): pl.pallas_call(kernel, out_shape=(pltpu.VMEM((RHS, QUARTER), F32),) * 3 +...  40.4 us
    unnamed x4, local copies, waits for them, and re-layouts  2.45 us

profile of v2, /device:TPU:1, one launch (start us, length us, event | category | flops | bytes accessed | tf_op | source)
XLA Modules:
  0.0 43.5 jit_solution(11977684587092270192)
XLA Ops:
  0.6 40.4 %cg_step.1 = (f32[16,768]{1,0:T(8,128)S(1)}, f32[16,768]{1,0:T(8,128)S(1)}, f32[16,768]{1,0:T(8,128)S(1)}, f32[8,16]{1,0:T(8,128)S(1)}) custom-call(s32[768,3072]{1,0:T(8,128)} %gen.1, s32[768,3072]{1,0:T(8,128)} %cal.1, s32[768,1024]{1,0:T(8,128)} %dos.1, s32[1,768]{1,0:T(1,128)} %order_in.1, f32[1,16]{1,0:T(1,128)} %bitcast.13, f32[16,768]{1,0:T(8,128)} %bitcast.10, ...), custom_call_target="tpu_custom_call" | custom-call | flops 400000000 | bytes 22000000 | tf_op jit(solution)/shard_map/cg_step/pallas_call | solution.py:391
  41.0 0.6 %copy.16 = f32[768,16]{0,1:T(8,128)} copy(f32[768,16]{0,1:T(8,128)S(1)} %bitcast.9) | data formatting | bytes 98304
  41.7 0.6 %copy.17 = f32[768,16]{0,1:T(8,128)} copy(f32[768,16]{0,1:T(8,128)S(1)} %bitcast.8) | data formatting | bytes 98304
  42.3 0.6 %copy.19 = f32[8,16]{1,0:T(8,128)} copy(f32[8,16]{1,0:T(8,128)S(1)} %get-tuple-element.15) | data formatting | bytes 1024
  42.9 0.6 %copy.18 = f32[768,16]{0,1:T(8,128)} copy(f32[768,16]{0,1:T(8,128)S(1)} %bitcast.7) | data formatting | bytes 98304

commit v3 on v2

--- a/solution.py
+++ b/solution.py
@@ -19,15 +19,16 @@
 BLK = 128
 NBLK = LOCAL // BLK
 WINDOW = 3
-EARLY = 3
 F32 = jnp.float32
 BF16 = jnp.bfloat16
 MESH = pl.DeviceIdType.MESH
 
 
 def owner_of(block, group):
-    far = block + 10 - 4 * lax.rem(block // 2, 2)
-    return 2 * (block + group * (far - block)) + group
+    turn = block + 2
+    first = lax.rem(turn, 4) + 4 * (1 - turn // 4)
+    second = block + 7
+    return 2 * (first + group * (second - first)) + group
 
 
 def rows_iota(shape):
@@ -102,6 +103,9 @@
         load(j, 1).start()
 
     barrier = pltpu.get_barrier_semaphore()
+    place = me // 8 + lax.rem(me // 2, 4) + 2 * z
+    ahead = jnp.maximum(3 - place // 2, 0)
+    early = jnp.maximum(6 - place // 3, 3)
 
     def greet(device):
         pl.semaphore_signal(barrier, inc=1, device_id=device, device_id_type=MESH)
@@ -124,6 +128,30 @@
     stat_s[...] = jnp.where(row8 == 2, pair, 0.0)
     g_acc[...] = jnp.zeros((RHS, WIDE), F32)
 
+    def convert_block(j):
+        load(j, 0).wait()
+        load(j, 1).wait()
+
+        @pl.when(j + WINDOW < NBLK)
+        def _():
+            load(j + WINDOW, 0).start()
+            load(j + WINDOW, 1).start()
+
+        @pl.when(j + WINDOW == NBLK)
+        def _():
+            load_dos.start()
+
+        def convert(i, carry):
+            first = pl.multiple_of(i * 16, 16)
+            called = cv[j, pl.ds(first, 16), :].astype(F32).astype(BF16)
+            codes = gv[j, pl.ds(first, 16), :].astype(F32).astype(BF16)
+            xb[j, pl.ds(first, 16), :] = codes * called
+            xb[j, pl.ds(pl.multiple_of(first + BLK, 16), 16), :] = called
+            return carry
+
+        lax.fori_loop(0, BLK // 16, convert, 0)
+
+    each_block(0, ahead, convert_block)
     pl.semaphore_wait(barrier, NP - 1 + NZ - 1)
 
     def direction_copy(k):
@@ -142,29 +170,6 @@
         return remote(
             rs_s.at[j, group], rs_r.at[slot], rs_send.at[j, group], rs_recv, {"var": z, "samp": owner}
         )
-
-    def convert_block(j):
-        load(j, 0).wait()
-        load(j, 1).wait()
-
-        @pl.when(j + WINDOW < NBLK)
-        def _():
-            load(j + WINDOW, 0).start()
-            load(j + WINDOW, 1).start()
-
-        @pl.when(j + WINDOW == NBLK)
-        def _():
-            load_dos.start()
-
-        def convert(i, carry):
-            first = pl.multiple_of(i * 16, 16)
-            called = cv[j, pl.ds(first, 16), :].astype(F32).astype(BF16)
-            codes = gv[j, pl.ds(first, 16), :].astype(F32).astype(BF16)
-            xb[j, pl.ds(first, 16), :] = codes * called
-            xb[j, pl.ds(pl.multiple_of(first + BLK, 16), 16), :] = called
-            return carry
-
-        lax.fori_loop(0, BLK // 16, convert, 0)
 
     def project_block(j, stats):
         proj = lax.dot_general(dx[...], xb[j], (((1,), (1,)), ((), ())), preferred_element_type=F32)
@@ -221,20 +226,20 @@
     def back_product(j, weights):
         g_acc[...] += jnp.dot(weights, xb[j], preferred_element_type=F32)
 
-    each_block(0, EARLY, convert_block)
+    each_block(ahead, early, convert_block)
     for k in range(1, NZ):
         stat_copy(k).wait()
     stats = stat_s[...] + stat_r[0] + stat_r[1] + stat_r[2]
     for k in range(1, NZ):
         direction_copy(k).wait()
-    each_block(0, EARLY, lambda j: project_block(j, stats))
+    each_block(0, early, lambda j: project_block(j, stats))
 
     def convert_and_project(j):
         convert_block(j)
         project_block(j, stats)
 
-    each_block(EARLY, NBLK, convert_and_project)
-    each_block(0, NBLK - 2, owner_part)
+    each_block(early, NBLK, convert_and_project)
+    each_block(0, NBLK, owner_part)
 
     load_dos.wait()
 
@@ -274,19 +279,8 @@
     for k in range(1, NZ):
         cz_copy(k).start()
 
-    each_block(NBLK - 2, NBLK, owner_part)
     each_block(0, NBLK - 1, lambda j: back_product(j, back(j)))
 
-    for k in range(1, NZ):
-        cz_copy(k).wait()
-    own = cz_s[:, pl.ds(pl.multiple_of(z * part, part), part)] + cz_r[0] + cz_r[1] + cz_r[2]
-    own = jnp.concatenate([own, jnp.zeros((128 - 40, part), F32)], axis=0)
-    cp_s[...] = jnp.transpose(own).reshape(NP, 8, 128)
-
-    def cp_copy(k):
-        return remote(cp_s.at[lax.rem(me + k, NP)], cp_r.at[k - 1], cp_send, cp_recv, p_peer(k))
-
-    each_plane_peer(lambda k: cp_copy(k).start())
     weights = back(NBLK - 1)
 
     for j in range(NBLK):
@@ -302,9 +296,6 @@
 
     for k in range(1, NZ):
         q_copy(k).start()
-    back_product(NBLK - 1, weights)
-    g_s[...] = (g_acc[...] * (1.0 / VARIANTS)).astype(BF16)
-
     def g_copy(k):
         peer = lax.rem(z + k, NZ)
         return remote(
@@ -312,8 +303,27 @@
             g_send.at[k - 1], g_recv.at[k - 1], z_peer(k),
         )
 
-    for k in range(1, NZ):
-        g_copy(k).start()
+    for k in (2, 1, 3, 0):
+        span = pl.ds(pl.multiple_of(lax.rem(z + k, NZ) * QUARTER, QUARTER), QUARTER)
+        g_part = (
+            g_acc[:, span] + jnp.dot(weights, xb[NBLK - 1, :, span], preferred_element_type=F32)
+        ) * (1.0 / VARIANTS)
+        if k:
+            g_s[:, span] = g_part.astype(BF16)
+            g_copy(k).start()
+        else:
+            own_g = g_part
+
+    for k in range(1, NZ):
+        cz_copy(k).wait()
+    own = cz_s[:, pl.ds(pl.multiple_of(z * part, part), part)] + cz_r[0] + cz_r[1] + cz_r[2]
+    own = jnp.concatenate([own, jnp.zeros((128 - 40, part), F32)], axis=0)
+    cp_s[...] = jnp.transpose(own).reshape(NP, 8, 128)
+
+    def cp_copy(k):
+        return remote(cp_s.at[lax.rem(me + k, NP)], cp_r.at[k - 1], cp_send, cp_recv, p_peer(k))
+
+    each_plane_peer(lambda k: cp_copy(k).start())
 
     for k in range(1, NZ):
         q_copy(k).wait()
@@ -328,7 +338,6 @@
     sol_new[...] = s_next
     s_sum = jnp.sum(s_next, axis=1, keepdims=True)
     s_square = jnp.sum(s_next * s_next, axis=1, keepdims=True)
-    own_g = g_acc[:, pl.ds(pl.multiple_of(z * QUARTER, QUARTER), QUARTER)] * (1.0 / VARIANTS)
     base = to_column(noise[...]) * d + own_g
     for k in range(1, NZ):
         g_copy(k).wait()
@@ -356,6 +365,24 @@
     dose_freq = (dose[:, 32:33] * (1.0 / 100.0) + 1.0) / (2.0 * SAMPLES + 2.0)
     dose_spread = jnp.sqrt(2.0 * dose_freq * (1.0 - dose_freq))
     cross_sum = dose[:, 0:RHS] + step_row * dose[:, RHS:2 * RHS]
+    pltpu.make_async_copy(cp_r, cp_r, cp_send).wait()
+
+    def sent(j, carry):
+        for group in range(2):
+            @pl.when(me != owner_of(j, group))
+            def _():
+                rs_copy(j, group).wait_send()
+
+            @pl.when(me == owner_of(j, group))
+            def _():
+                view = rs_r.at[:, pl.ds(0, 8), :]
+                pltpu.make_async_copy(view, view, ag_send).wait()
+                pltpu.make_async_copy(d2_r, d2_r, sq_send).wait()
+
+        return carry
+
+    lax.fori_loop(0, NBLK, sent, 0)
+
     pltpu.make_async_copy(d2_r, d2_r, d2_recv).wait()
     sums = d2_s[...] + jnp.sum(d2_r[...], axis=0)
     beta = to_column(sums[:, 0:RHS] / (res_norm + 1e-6))
@@ -364,23 +391,15 @@
     scores[...] = (cross_sum * (1.0 / 100.0) - 2.0 * dose_freq * sums[:, RHS:2 * RHS]) / (dose_spread * scale)
 
     pltpu.make_async_copy(d2_r, d2_r, d2_send).wait()
-    pltpu.make_async_copy(cp_r, cp_r, cp_send).wait()
-
-    def sent(j, carry):
-        for group in range(2):
-            @pl.when(me != owner_of(j, group))
-            def _():
-                rs_copy(j, group).wait_send()
-
-            @pl.when(me == owner_of(j, group))
-            def _():
-                view = rs_r.at[:, pl.ds(0, 8), :]
-                pltpu.make_async_copy(view, view, ag_send).wait()
-                pltpu.make_async_copy(d2_r, d2_r, sq_send).wait()
-
-        return carry
-
-    lax.fori_loop(0, NBLK, sent, 0)
+
+
+def store_kernel(*refs):
+    held, results, sem = refs[:4], refs[4:8], refs[8]
+    copies = [pltpu.make_async_copy(held[i], results[i], sem.at[i]) for i in range(4)]
+    for copy in copies:
+        copy.start()
+    for copy in copies:
+        copy.wait()
 
 
 def body(genotypes, called, dosage, sample_order, noise_ratio, solution, residual, direction):
@@ -448,7 +467,16 @@
         genotypes, called, dosage, sample_order, noise_ratio.reshape(1, RHS),
         solution.T, residual.T, direction.T,
     )
-    sol_new, res_new, dir_new, scores = outs
+    outs = [pltpu.with_memory_space_constraint(out, pltpu.VMEM) for out in outs]
+    sol_new, res_new, dir_new, scores = pl.pallas_call(
+        store_kernel,
+        out_shape=(small, small, small, jax.ShapeDtypeStruct((8, RHS), F32)),
+        in_specs=[vmem] * 4,
+        out_specs=(hbm,) * 4,
+        scratch_shapes=[dma((4,))],
+        cost_estimate=pl.CostEstimate(flops=0, bytes_accessed=300_000, transcendentals=0),
+        name="store",
+    )(*outs)
     return (sol_new.T, res_new.T, dir_new.T, scores)
 
 

time: 43.6 us -> 40.4 us (0.927)
  local copies, waits for them, and re-layouts: 2.45 us -> 0 us
  Pallas kernels: 40.4 us -> 39.6 us
    unnamed x4 -> x0, local copies, waits for them, and re-layouts: 2.45 us -> none
    pallas_call x1, Pallas kernels: 40.4 us -> 39 us  [body(): pl.pallas_call(kernel, out_shape=(pltpu.VMEM((RHS, QUARTER), F32),) * 3 +...]
    pallas_call x0 -> x1, Pallas kernels: none -> 0.69 us  [body(): pl.pallas_call(store_kernel, out_shape=(small, small, small, jax.ShapeDty...]
where the time goes in v3:
time: 40.4 us; the launch traced here: 40.3 us
  Pallas kernels  39.6 us (98%)
  between operations  0.64 us (2%)
    pallas_call x1, Pallas kernels, body(): pl.pallas_call(kernel, out_shape=(pltpu.VMEM((RHS, QUARTER), F32),) * 3 +...  39 us

profile of v3, /device:TPU:1, one launch (start us, length us, event | category | flops | bytes accessed | tf_op | source)
XLA Modules:
  0.0 40.3 jit_solution(3249499059443708667)
XLA Ops:
  0.6 39.0 %cg_step.1 = (f32[16,768]{1,0:T(8,128)S(1)}, f32[16,768]{1,0:T(8,128)S(1)}, f32[16,768]{1,0:T(8,128)S(1)}, f32[8,16]{1,0:T(8,128)S(1)}) custom-call(s32[768,3072]{1,0:T(8,128)} %gen.1, s32[768,3072]{1,0:T(8,128)} %cal.1, s32[768,1024]{1,0:T(8,128)} %dos.1, s32[1,768]{1,0:T(1,128)} %order_in.1, f32[1,16]{1,0:T(1,128)} %bitcast.10, f32[16,768]{1,0:T(8,128)} %bitcast.7, ...), custom_call_target="tpu_custom_call" | custom-call | flops 400000000 | bytes 22000000 | tf_op jit(solution)/shard_map/cg_step/pallas_call | solution.py:410
  39.6 0.7 %store.1 = (f32[16,768]{1,0:T(8,128)}, f32[16,768]{1,0:T(8,128)}, f32[16,768]{1,0:T(8,128)}, f32[8,16]{1,0:T(8,128)}) custom-call(f32[16,768]{1,0:T(8,128)S(1)} %get-tuple-element.12.refs_0_, f32[16,768]{1,0:T(8,128)S(1)} %get-tuple-element.13.refs_1_, f32[16,768]{1,0:T(8,128)S(1)} %get-tuple-element.14.refs_2_, f32[8,16]{1,0:T(8,128)S(1)} %get-tuple-element.15.refs_3_), custom_call_target="tpu_custom_call" | custom-call | bytes 300000 | tf_op jit(solution)/shard_map/store/pallas_call | solution.py:471

commit v4 on v3

--- a/solution.py
+++ b/solution.py
@@ -67,15 +67,19 @@
     def z_peer(k):
         return {"var": lax.rem(z + k, NZ), "samp": me}
 
+    def beside(k):
+        peer = me + k
+        return jnp.where(peer >= NP, peer - NP, peer)
+
     def p_peer(k):
-        return {"var": z, "samp": lax.rem(me + k, NP)}
+        return {"var": z, "samp": beside(k)}
 
     def each_block(first, last, work):
         lax.fori_loop(first, last, lambda j, carry: (work(j), carry)[1], 0)
 
     def each_plane_peer(send):
         for first in (16, 8, 24, 0):
-            lax.fori_loop(max(first, 1), first + 8, lambda k, carry: (send(k), carry)[1], 0)
+            lax.fori_loop(max(first, 1), first + 8, lambda k, carry: (send(k), carry)[1], 0, unroll=True)
 
     def remote(src, dst, send, recv, device):
         return pltpu.make_async_remote_copy(
@@ -105,7 +109,7 @@
     barrier = pltpu.get_barrier_semaphore()
     place = me // 8 + lax.rem(me // 2, 4) + 2 * z
     ahead = jnp.maximum(3 - place // 2, 0)
-    early = jnp.maximum(6 - place // 3, 3)
+    early = NBLK - z
 
     def greet(device):
         pl.semaphore_signal(barrier, inc=1, device_id=device, device_id_type=MESH)
@@ -137,7 +141,7 @@
             load(j + WINDOW, 0).start()
             load(j + WINDOW, 1).start()
 
-        @pl.when(j + WINDOW == NBLK)
+        @pl.when(j == NBLK - 1)
         def _():
             load_dos.start()
 
@@ -321,7 +325,7 @@
     cp_s[...] = jnp.transpose(own).reshape(NP, 8, 128)
 
     def cp_copy(k):
-        return remote(cp_s.at[lax.rem(me + k, NP)], cp_r.at[k - 1], cp_send, cp_recv, p_peer(k))
+        return remote(cp_s.at[beside(k)], cp_r.at[k - 1], cp_send, cp_recv, p_peer(k))
 
     each_plane_peer(lambda k: cp_copy(k).start())
 

time: 40.4 us -> 40.1 us (level)
  no operation moved by 1% of the time
where the time goes in v4:
time: 40.1 us; the launch traced here: 39.9 us
  Pallas kernels  39.3 us (98%)
  between operations  0.64 us (2%)
    pallas_call x1, Pallas kernels, body(): pl.pallas_call(kernel, out_shape=(pltpu.VMEM((RHS, QUARTER), F32),) * 3 +...  38.6 us

profile of v4, /device:TPU:1, one launch (start us, length us, event | category | flops | bytes accessed | tf_op | source)
XLA Modules:
  0.0 39.9 jit_solution(9781406468838772380)
XLA Ops:
  0.6 38.6 %cg_step.1 = (f32[16,768]{1,0:T(8,128)S(1)}, f32[16,768]{1,0:T(8,128)S(1)}, f32[16,768]{1,0:T(8,128)S(1)}, f32[8,16]{1,0:T(8,128)S(1)}) custom-call(s32[768,3072]{1,0:T(8,128)} %gen.1, s32[768,3072]{1,0:T(8,128)} %cal.1, s32[768,1024]{1,0:T(8,128)} %dos.1, s32[1,768]{1,0:T(1,128)} %order_in.1, f32[1,16]{1,0:T(1,128)} %bitcast.10, f32[16,768]{1,0:T(8,128)} %bitcast.7, ...), custom_call_target="tpu_custom_call" | custom-call | flops 400000000 | bytes 22000000 | tf_op jit(solution)/shard_map/cg_step/pallas_call | solution.py:414
  39.3 0.7 %store.1 = (f32[16,768]{1,0:T(8,128)}, f32[16,768]{1,0:T(8,128)}, f32[16,768]{1,0:T(8,128)}, f32[8,16]{1,0:T(8,128)}) custom-call(f32[16,768]{1,0:T(8,128)S(1)} %get-tuple-element.12.refs_0_, f32[16,768]{1,0:T(8,128)S(1)} %get-tuple-element.13.refs_1_, f32[16,768]{1,0:T(8,128)S(1)} %get-tuple-element.14.refs_2_, f32[8,16]{1,0:T(8,128)S(1)} %get-tuple-element.15.refs_3_), custom_call_target="tpu_custom_call" | custom-call | bytes 300000 | tf_op jit(solution)/shard_map/store/pallas_call | solution.py:475

commit v5 on v4

--- a/solution.py
+++ b/solution.py
@@ -236,13 +236,15 @@
     stats = stat_s[...] + stat_r[0] + stat_r[1] + stat_r[2]
     for k in range(1, NZ):
         direction_copy(k).wait()
-    each_block(0, early, lambda j: project_block(j, stats))
 
     def convert_and_project(j):
-        convert_block(j)
+        @pl.when(j >= early)
+        def _():
+            convert_block(j)
+
         project_block(j, stats)
 
-    each_block(early, NBLK, convert_and_project)
+    each_block(0, NBLK, convert_and_project)
     each_block(0, NBLK, owner_part)
 
     load_dos.wait()

time: 40.1 us -> 40.1 us (level)
  no operation moved by 1% of the time
where the time goes in v5:
time: 40.1 us; the launch traced here: 40 us
  Pallas kernels  39.3 us (98%)
  between operations  0.64 us (2%)
    pallas_call x1, Pallas kernels, body(): pl.pallas_call(kernel, out_shape=(pltpu.VMEM((RHS, QUARTER), F32),) * 3 +...  38.6 us

profile of v5, /device:TPU:1, one launch (start us, length us, event | category | flops | bytes accessed | tf_op | source)
XLA Modules:
  0.0 40.0 jit_solution(545622374934498058)
XLA Ops:
  0.6 38.6 %cg_step.1 = (f32[16,768]{1,0:T(8,128)S(1)}, f32[16,768]{1,0:T(8,128)S(1)}, f32[16,768]{1,0:T(8,128)S(1)}, f32[8,16]{1,0:T(8,128)S(1)}) custom-call(s32[768,3072]{1,0:T(8,128)} %gen.1, s32[768,3072]{1,0:T(8,128)} %cal.1, s32[768,1024]{1,0:T(8,128)} %dos.1, s32[1,768]{1,0:T(1,128)} %order_in.1, f32[1,16]{1,0:T(1,128)} %bitcast.10, f32[16,768]{1,0:T(8,128)} %bitcast.7, ...), custom_call_target="tpu_custom_call" | custom-call | flops 400000000 | bytes 22000000 | tf_op jit(solution)/shard_map/cg_step/pallas_call | solution.py:416
  39.3 0.7 %store.1 = (f32[16,768]{1,0:T(8,128)}, f32[16,768]{1,0:T(8,128)}, f32[16,768]{1,0:T(8,128)}, f32[8,16]{1,0:T(8,128)}) custom-call(f32[16,768]{1,0:T(8,128)S(1)} %get-tuple-element.12.refs_0_, f32[16,768]{1,0:T(8,128)S(1)} %get-tuple-element.13.refs_1_, f32[16,768]{1,0:T(8,128)S(1)} %get-tuple-element.14.refs_2_, f32[8,16]{1,0:T(8,128)S(1)} %get-tuple-element.15.refs_3_), custom_call_target="tpu_custom_call" | custom-call | bytes 300000 | tf_op jit(solution)/shard_map/store/pallas_call | solution.py:477
